TPU v7x, 256 devices: a whole 4x4x8 slice. The times are simulated.
256 devices in a mesh: sec: 2 (over y_hi), tile: 128 (over z, x, y_lo, core).
Axes of the slice: x: 4, y: 4 (y_hi: 2, y_lo: 2; y = y_hi * 2 + y_lo), z: 8, core: 2. Of those that a mesh axis runs over, the one named last changes fastest.
Arguments:
- atm_fields: bfloat16 [128, 1048576], P(None, ('sec', 'tile')), may hold values from -6 to 6
- remap_blocks: bfloat16 [16384, 4, 128, 128], P(('sec', 'tile')), may hold values from -0.25 to 0.25
- block_cols: int32 [16384, 4], P(('sec', 'tile')), may hold values from 0 to 8191, as said below
- flux_coef: float32 [32], replicated, may hold values from -1 to 1
- ocean_temp: float32 [1024, 2048], P(('sec', 'tile')), may hold values from -6 to 6
- sea_mask: int32 [1024, 2048], P(('sec', 'tile')), may hold values 0 or 1
Outputs:
- ocean_fields: bfloat16 [128, 2097152], P(None, ('sec', 'tile'))
- final_temp: float32 [1024, 2048], P(('sec', 'tile'))
Inputs may be any that keep to these rules, and one draw needn't show every extreme that they name: `block_cols`: counting devices over sec+tile in order, an ocean tile of device d names only atmosphere tiles of devices d - 1, d and d + 1, that is tiles (32 (d - 1)) to (32 (d + 2) - 1).
All inputs are finite; a program needn't handle non-finite values. No bound on the sum of `sea_mask` on one device may be relied on, other than what follows from the above.
Results may differ from a plain program's by a relative error of at most 0.006.
Values may be sent and summed in bfloat16 or wider, within the bound.
A program may use at most 64 MiB of HBM per device.

v0:
```python
import jax
import jax.numpy as jnp
from jax import lax
from jax.sharding import PartitionSpec as P

DIFFUSE = 0.24
TIMESTEP = 0.5
RESTORE = 0.5


def extended(shard, sides, width):
    for axis, dim in sides:
        peers, length = (lax.axis_size(axis), shard.shape[dim])
        up = [(i, (i + 1) % peers) for i in range(peers - 1)]
        down = [(j, i) for i, j in up]
        last = lax.slice_in_dim(shard, length - width, length, axis=dim)
        first = lax.slice_in_dim(shard, 0, width, axis=dim)
        before = lax.ppermute(last, axis, up)
        after = lax.ppermute(first, axis, down)
        shard = jnp.concatenate([before, shard, after], axis=dim)
    return shard


def shortened(shard):

    def short(part):
        return part.astype(jnp.bfloat16) if part.dtype == jnp.float32 else part

    return jax.tree.map(short, shard)


def sweep(padded, mask_pad, forcing, air_temp):
    centre = padded[1:-1]
    mask_mid = mask_pad[1:-1]

    def facing(other, other_mask):
        return other_mask * other + (1.0 - other_mask) * centre

    north = facing(padded[2:], mask_pad[2:])
    south = facing(padded[:-2], mask_pad[:-2])
    east = facing(jnp.roll(centre, -1, 1), jnp.roll(mask_mid, -1, 1))
    west = facing(jnp.roll(centre, 1, 1), jnp.roll(mask_mid, 1, 1))
    lap = north + south + east + west - 4.0 * centre
    return centre + mask_mid * (
        DIFFUSE * lap + TIMESTEP * forcing - TIMESTEP * RESTORE * (centre - air_temp)
    )


def body(atm_fields, remap_blocks, block_cols, flux_coef, ocean_temp, sea_mask):
    rows_n = atm_fields.shape[0]
    atm_count = atm_fields.shape[1] // 128
    ocean_count = block_cols.shape[0]
    slots = block_cols.shape[1]
    band_rows = ocean_temp.shape[0]
    columns_n = ocean_temp.shape[1]
    fields_n = flux_coef.shape[0]
    sweeps = rows_n // fields_n // 2
    device = lax.axis_index(("sec", "tile"))
    window = extended(atm_fields, ((("sec", "tile"), 1),), atm_fields.shape[1])
    atm_tiles = window.reshape(rows_n, 3 * atm_count, 128).transpose(1, 0, 2)
    local_cols = block_cols - (device - 1) * atm_count
    picked = jnp.take(atm_tiles, local_cols.reshape(-1), axis=0)
    picked = picked.reshape(ocean_count, slots, rows_n, 128)
    remapped = jnp.einsum(
        "tkrc,tkco->rto", picked, remap_blocks, preferred_element_type=jnp.float32
    )
    remapped = remapped.reshape(rows_n, ocean_count * 128)
    ocean_fields = remapped.astype(jnp.bfloat16)
    fields = remapped.reshape(rows_n // fields_n, fields_n, band_rows, columns_n)
    net_heat = jnp.einsum("f,jfyx->jyx", flux_coef, fields, precision=lax.Precision.HIGHEST)
    forcing = 0.5 * (net_heat[0::2] + net_heat[1::2])
    air_temp = 0.5 * (fields[0::2, 0] + fields[1::2, 0])
    sea = sea_mask.astype(jnp.float32)
    temp = ocean_temp
    mask_pad = sea
    for step in range(sweeps):
        if step == 0:
            both = extended(
                jnp.stack([temp, sea]).astype(jnp.bfloat16), ((("sec", "tile"), 1),), 1
            ).astype(jnp.float32)
            padded = both[0]
            mask_pad = both[1]
        else:
            padded = extended(shortened(temp), ((("sec", "tile"), 0),), 1).astype(temp.dtype)
        temp = sweep(padded, mask_pad, forcing[step], air_temp[step])
    return (ocean_fields, temp)


def solution(mesh):
    placed = (
        P(None, ("sec", "tile")),
        P(("sec", "tile"), None, None, None),
        P(("sec", "tile"), None),
        P(),
        P(("sec", "tile"), None),
        P(("sec", "tile"), None),
    )
    return jax.shard_map(
        body,
        mesh=mesh,
        in_specs=placed,
        out_specs=(P(None, ("sec", "tile")), P(("sec", "tile"), None)),
        check_vma=False,
    )
```

profile of v0, /device:TPU:16, one launch (start us, length us, event | category | flops | bytes accessed | tf_op | source)
XLA Modules:
  0.0 100.2 jit_solution(12500131049839135886)
XLA Ops:
  0.6 1.6 %copy.20 = bf16[128,4096]{0,1:T(8,128)(2,1)S(1)} copy(bf16[128,4096]{1,0:T(8,128)(2,1)} %param.6) | data formatting | bytes 2097152 | tf_op args[0]
  2.3 9.3 %collective-permute-start.1 = (bf16[128,4096]{0,1:T(8,128)(2,1)S(1)}, bf16[128,4096]{0,1:T(8,128)(2,1)S(1)}, u32[]{:S(2)}, u32[]{:S(2)}) collective-permute-start(bf16[128,4096]{0,1:T(8,128)(2,1)S(1)} %copy.20), channel_id=1, source_target_pairs={{1,0},{2,1},{3,2},{4,3},{5,4},{6,5},{7,6},{8,7},{9,8},{10,9},{11,1... | collective-permute-start | bytes 3145736 | tf_op jit(solution)/shard_map/ppermute | solution.py:19
  11.6 1.9 %collective-permute-start = (bf16[128,4096]{0,1:T(8,128)(2,1)S(1)}, bf16[128,4096]{0,1:T(8,128)(2,1)S(1)}, u32[]{:S(2)}, u32[]{:S(2)}) collective-permute-start(bf16[128,4096]{0,1:T(8,128)(2,1)S(1)} %copy.20), channel_id=1, source_target_pairs={{0,1},{1,2},{2,3},{3,4},{4,5},{5,6},{6,7},{7,8},{8,9},{9,10},{10,1... | collective-permute-start | bytes 3145736 | tf_op jit(solution)/shard_map/ppermute | solution.py:18
  13.5 0.8 convert_bitcast_fusion
  14.3 0.8 fusion.44
  15.1 7.9 %collective-permute-start.3 = (bf16[2,1,2048]{2,1,0:T(2,128)(2,1)S(1)}, bf16[2,1,2048]{2,1,0:T(2,128)(2,1)S(1)}, u32[]{:S(2)}, u32[]{:S(2)}) collective-permute-start(bf16[2,1,2048]{2,1,0:T(2,128)(2,1)S(1)} %get-tuple-element.25), channel_id=1, source_target_pairs={{1,0},{2,1},{3,2},{4,3},{5,4},{6,5},{7,6},{8,7},{9,8},{10,9},{11,1... | collective-permute-start | bytes 24584 | tf_op jit(solution)/shard_map/ppermute | solution.py:19
  22.9 1.9 %collective-permute-start.2 = (bf16[2,1,2048]{2,1,0:T(2,128)(2,1)S(1)}, bf16[2,1,2048]{2,1,0:T(2,128)(2,1)S(1)}, u32[]{:S(2)}, u32[]{:S(2)}) collective-permute-start(bf16[2,1,2048]{2,1,0:T(2,128)(2,1)S(1)} %get-tuple-element.24), channel_id=1, source_target_pairs={{0,1},{1,2},{2,3},{3,4},{4,5},{5,6},{6,7},{7,8},{8,9},{9,10},{10,1... | collective-permute-start | bytes 24584 | tf_op jit(solution)/shard_map/ppermute | solution.py:18
  24.9 0.7 compare_and_fusion
  25.8 0.1 copy.19
  25.9 6.3 %collective-permute-done.2 = bf16[2,1,2048]{2,1,0:T(2,128)(2,1)S(1)} collective-permute-done((bf16[2,1,2048]{2,1,0:T(2,128)(2,1)S(1)}, bf16[2,1,2048]{2,1,0:T(2,128)(2,1)S(1)}, u32[]{:S(2)}, u32[]{:S(2)}) %collective-permute-start.2) | collective-permute-done | bytes 8224 | tf_op jit(solution)/shard_map/ppermute | solution.py:18
  32.5 16.4 %pad_maximum_fusion = bf16[128,12288]{0,1:T(8,128)(2,1)} fusion(bf16[128,4096]{0,1:T(8,128)(2,1)S(1)} %collective-permute-done.1, bf16[128,4096]{0,1:T(8,128)(2,1)S(1)} %copy.20, bf16[128,4096]{0,1:T(8,128)(2,1)S(1)} %collective-permute-done), kind=kLoop, calls=%fused_computation.7 | loop fusion | flops 9437184 | bytes 6291456 | tf_op jit(solution)/shard_map/concatenate | solution.py:20
  48.9 3.5 %copy.23 = bf16[128,96,128]{2,0,1:T(8,128)(2,1)S(1)} copy(bf16[128,96,128]{0,2,1:T(8,128)(2,1)} %bitcast.110) | data formatting | bytes 6291456 | tf_op jit(solution)/shard_map/reshape | solution.py:60
  52.4 8.6 %gather_fusion = bf16[256,128,128]{2,1,0:T(8,128)(2,1)} fusion(bf16[96,128,128]{2,1,0:T(8,128)(2,1)S(1)} %bitcast.109, s32[1024]{0:T(1024)S(1)} %pad_clamp_fusion), kind=kCustom, calls=%fused_computation | custom fusion | bytes 16778240 | tf_op jit(solution)/shard_map/jit(_take)/gather | solution.py:62
  61.0 8.7 %fusion.54 = (bf16[128,64,128]{0,2,1:T(8,128)(2,1)S(1)}, f32[128,64,128]{0,2,1:T(8,128)}) fusion(bf16[64,4,128,128]{3,2,1,0:T(8,128)(2,1)} %param.7, bf16[64,4,128,128]{3,2,1,0:T(8,128)(2,1)} %bitcast.111, pred[64,4]{1,0:T(8,128)(4,1)S(1)} %copy.19), kind=kOutput, calls=%fused_computation.89 | convolution fusion | flops 1078984704 | bytes 23068928 | tf_op jit(solution)/shard_map/tkrc,tkco->rto/dot_general | solution.py:64
  69.8 5.4 %copy.26 = f32[128,64,128]{2,1,0:T(8,128)} copy(f32[128,64,128]{0,2,1:T(8,128)} %get-tuple-element.29) | data formatting | bytes 8388608 | tf_op jit(solution)/shard_map/tkrc,tkco->rto/transpose | solution.py:64
  75.1 5.3 %reshape_reshape.3 = f32[4,32,4,2048]{3,2,1,0:T(4,128)} reshape(f32[128,64,128]{2,1,0:T(8,128)} %copy.26) | data formatting | bytes 8388608 | tf_op jit(solution)/shard_map/reshape;reshape | solution.py:69
  80.4 0.9 add_multiply_fusion
  81.3 6.6 %fusion.3 = f32[1,4,4,2048]{3,0,2,1:T(1,128)S(1)} fusion(f32[4,32,4,2048]{3,2,1,0:T(4,128)} %reshape_reshape.3, f32[32]{0:T(128)S(1)} %copy-done), kind=kOutput, calls=%fused_computation.4 | convolution fusion | flops 12582912 | bytes 4325504 | tf_op jit(solution)/shard_map/f,jfyx->jyx/dot_general | solution.py:70
  88.0 0.1 fusion.28
  88.1 1.9 %collective-permute-start.5 = (bf16[1,2048]{1,0:T(2,128)(2,1)S(1)}, bf16[1,2048]{1,0:T(2,128)(2,1)S(1)}, u32[]{:S(2)}, u32[]{:S(2)}) collective-permute-start(bf16[1,2048]{1,0:T(2,128)(2,1)S(1)} %get-tuple-element.27), channel_id=1, source_target_pairs={{1,0},{2,1},{3,2},{4,3},{5,4},{6,5},{7,6},{8,7},{9,8},{10,9},{11,1... | collective-permute-start | bytes 12296 | tf_op jit(solution)/shard_map/ppermute | solution.py:19
  90.1 2.4 %collective-permute-start.4 = (bf16[1,2048]{1,0:T(2,128)(2,1)S(1)}, bf16[1,2048]{1,0:T(2,128)(2,1)S(1)}, u32[]{:S(2)}, u32[]{:S(2)}) collective-permute-start(bf16[1,2048]{1,0:T(2,128)(2,1)S(1)} %get-tuple-element.26), channel_id=1, source_target_pairs={{0,1},{1,2},{2,3},{3,4},{4,5},{5,6},{6,7},{7,8},{8,9},{9,10},{10,1... | collective-permute-start | bytes 12296 | tf_op jit(solution)/shard_map/ppermute | solution.py:18
  92.5 2.9 %copy.27 = bf16[128,8192]{1,0:T(8,128)(2,1)} copy(bf16[128,8192]{0,1:T(8,128)(2,1)S(1)} %bitcast.112) | data formatting | bytes 4194304
  95.4 3.9 %collective-permute-done.4 = bf16[1,2048]{1,0:T(2,128)(2,1)S(1)} collective-permute-done((bf16[1,2048]{1,0:T(2,128)(2,1)S(1)}, bf16[1,2048]{1,0:T(2,128)(2,1)S(1)}, u32[]{:S(2)}, u32[]{:S(2)}) %collective-permute-start.4) | collective-permute-done | bytes 4128 | tf_op jit(solution)/shard_map/ppermute | solution.py:18
  99.5 0.7 fusion.13
  (21 shorter events, 0.8 us)
Async XLA Ops:
  0.6 80.7 %copy-start = (f32[32]{0:T(128)S(1)}, f32[32]{0:T(128)}, u32[]{:S(2)}) copy-start(f32[32]{0:T(128)} %param.9) | copy-start | bytes 388
  2.3 30.2 %collective-permute-start.1 = (bf16[128,4096]{0,1:T(8,128)(2,1)S(1)}, bf16[128,4096]{0,1:T(8,128)(2,1)S(1)}, u32[]{:S(2)}, u32[]{:S(2)}) collective-permute-start(bf16[128,4096]{0,1:T(8,128)(2,1)S(1)} %copy.20), channel_id=1, source_target_pairs={{1,0},{2,1},{3,2},{4,3},{5,4},{6,5},{7,6},{8,7},{9,8},{10,9},{11,1... | collective-permute-start | bytes 3145736 | tf_op jit(solution)/shard_map/ppermute | solution.py:19
  11.6 20.9 %collective-permute-start = (bf16[128,4096]{0,1:T(8,128)(2,1)S(1)}, bf16[128,4096]{0,1:T(8,128)(2,1)S(1)}, u32[]{:S(2)}, u32[]{:S(2)}) collective-permute-start(bf16[128,4096]{0,1:T(8,128)(2,1)S(1)} %copy.20), channel_id=1, source_target_pairs={{0,1},{1,2},{2,3},{3,4},{4,5},{5,6},{6,7},{7,8},{8,9},{9,10},{10,1... | collective-permute-start | bytes 3145736 | tf_op jit(solution)/shard_map/ppermute | solution.py:18
  15.1 10.8 %collective-permute-start.3 = (bf16[2,1,2048]{2,1,0:T(2,128)(2,1)S(1)}, bf16[2,1,2048]{2,1,0:T(2,128)(2,1)S(1)}, u32[]{:S(2)}, u32[]{:S(2)}) collective-permute-start(bf16[2,1,2048]{2,1,0:T(2,128)(2,1)S(1)} %get-tuple-element.25), channel_id=1, source_target_pairs={{1,0},{2,1},{3,2},{4,3},{5,4},{6,5},{7,6},{8,7},{9,8},{10,9},{11,1... | collective-permute-start | bytes 24584 | tf_op jit(solution)/shard_map/ppermute | solution.py:19
  22.9 9.3 %collective-permute-start.2 = (bf16[2,1,2048]{2,1,0:T(2,128)(2,1)S(1)}, bf16[2,1,2048]{2,1,0:T(2,128)(2,1)S(1)}, u32[]{:S(2)}, u32[]{:S(2)}) collective-permute-start(bf16[2,1,2048]{2,1,0:T(2,128)(2,1)S(1)} %get-tuple-element.24), channel_id=1, source_target_pairs={{0,1},{1,2},{2,3},{3,4},{4,5},{5,6},{6,7},{7,8},{8,9},{9,10},{10,1... | collective-permute-start | bytes 24584 | tf_op jit(solution)/shard_map/ppermute | solution.py:18
  88.1 7.2 %collective-permute-start.5 = (bf16[1,2048]{1,0:T(2,128)(2,1)S(1)}, bf16[1,2048]{1,0:T(2,128)(2,1)S(1)}, u32[]{:S(2)}, u32[]{:S(2)}) collective-permute-start(bf16[1,2048]{1,0:T(2,128)(2,1)S(1)} %get-tuple-element.27), channel_id=1, source_target_pairs={{1,0},{2,1},{3,2},{4,3},{5,4},{6,5},{7,6},{8,7},{9,8},{10,9},{11,1... | collective-permute-start | bytes 12296 | tf_op jit(solution)/shard_map/ppermute | solution.py:19
  90.1 9.2 %collective-permute-start.4 = (bf16[1,2048]{1,0:T(2,128)(2,1)S(1)}, bf16[1,2048]{1,0:T(2,128)(2,1)S(1)}, u32[]{:S(2)}, u32[]{:S(2)}) collective-permute-start(bf16[1,2048]{1,0:T(2,128)(2,1)S(1)} %get-tuple-element.26), channel_id=1, source_target_pairs={{0,1},{1,2},{2,3},{3,4},{4,5},{5,6},{6,7},{7,8},{8,9},{9,10},{10,1... | collective-permute-start | bytes 12296 | tf_op jit(solution)/shard_map/ppermute | solution.py:18
where the time goes:
time: 101 us; the launch traced here: 100 us
  local copies, waits for them, and re-layouts  27.9 us (28%)
  starting transfers between devices  25.3 us (25%)
  other arithmetic  20.6 us (20%)
  matrix products  15.3 us (15%)
  waiting for transfers between devices  10.2 us (10%)
    ppermute x3, starting transfers between devices, extended(): after = lax.ppermute(first, axis, down)  19.1 us
    concatenate x1, other arithmetic, extended(): shard = jnp.concatenate([before, shard, after], axis=dim)  16.4 us
    ppermute x3, waiting for transfers between devices, extended(): before = lax.ppermute(last, axis, up)  10.2 us
    dot_general x1, matrix products, body(): jnp.einsum('tkrc,tkco->rto', picked, remap_blocks, preferred_element_type...  8.75 us
    gather x1, local copies, waits for them, and re-layouts, body(): picked = jnp.take(atm_tiles, local_cols.reshape(-1), axis=0)  8.61 us
    dot_general x1, matrix products, body(): jnp.einsum('f,jfyx->jyx', flux_coef, fields, precision=lax.Precision.HIGH...  6.56 us
    ppermute x3, starting transfers between devices, extended(): before = lax.ppermute(last, axis, up)  6.25 us
    transpose x1, local copies, waits for them, and re-layouts, body(): jnp.einsum('tkrc,tkco->rto', picked, remap_blocks, preferred_element_type...  5.4 us
  transfers between devices with their start and end apart: 6, of which 2 were waited for; matrix products, arithmetic and copies ran while one was open for 6% of the time, Pallas kernels for 0%

commit v1 on v0

v1 whole, which is shorter than its diff:
```python
import functools

import jax
import jax.numpy as jnp
from jax import lax
from jax.experimental import pallas as pl
from jax.experimental.pallas import tpu as pltpu
from jax.sharding import PartitionSpec as P

MESH = pl.DeviceIdType.MESH
DIFFUSE = 0.24
TIMESTEP = 0.5
RESTORE = 0.5
CHUNKS = (32, 32, 32, 16, 16)
STARTS = tuple(sum(CHUNKS[:j]) for j in range(len(CHUNKS)))
EARLY = len(CHUNKS) - 1
HALF = 2
WEIGHT_PARTS = 4
LANES = 128


def fill_coef(coef, flux_ref):
    for f in range(coef.shape[0]):
        coef[f : f + 1, :] = jnp.full((1, LANES), 0.5 * flux_ref[f], jnp.float32)


def remap_rows(rows, first, across, bands, cols_ref, window, weights, coef, store, forcing, air):
    slots = cols_ref.shape[0]

    def column(xt, carry):
        heat, warm = [], []
        for y in range(bands):
            t = y * across + xt
            picked = jnp.concatenate(
                [
                    window[:, pl.ds(cols_ref[k, t] * LANES, LANES)]
                    for k in range(slots)
                ],
                axis=1,
            )
            total = jnp.dot(picked, weights[t], preferred_element_type=jnp.float32)
            store(t, total.astype(jnp.bfloat16))
            heat.append(jnp.sum(total * coef[first : first + rows, :], axis=0, keepdims=True))
            if first == 0:
                warm.append(0.5 * total[0:1, :])
        lanes = pl.ds(pl.multiple_of(xt * LANES, LANES), LANES)
        top = jnp.zeros((1, LANES), jnp.float32)
        low = jnp.zeros((8 - 1 - bands, LANES), jnp.float32)
        forcing[:, lanes] += jnp.concatenate([top] + heat + [low], axis=0)
        if first == 0:
            air[:, lanes] += jnp.concatenate([top] + warm + [low], axis=0)
        return carry

    lax.fori_loop(0, across, column, 0, unroll=across)


def sweep(centre, sea, masks, forcing, air):
    columns_n = centre.shape[1]
    lap = (
        masks[0] * (pltpu.roll(centre, 7, 0) - centre)
        + masks[1] * (pltpu.roll(centre, 1, 0) - centre)
        + masks[2] * (pltpu.roll(centre, columns_n - 1, 1) - centre)
        + masks[3] * (pltpu.roll(centre, 1, 1) - centre)
    )
    return centre + sea * (
        DIFFUSE * lap + TIMESTEP * forcing - TIMESTEP * RESTORE * (centre - air)
    )


def exchange_kernel(
    secs, tiles, fields_n, cols_hbm, flux_hbm, atm_ref, blocks_ref, temp_hbm, sea_hbm,
    weights, ocean, last, temp, sea, masks, forcing1, air1, coef, cols_ref,
    named_ref, flux_ref, temp_ref, sea_ref, windows, forcing0, air0,
    edge_out, edge_in, edge2_out, edge2_in,
    small_sem, own_sem, weight_sem, bulk_send, bulk_recv, edge_send, edge_recv, turn_sem,
):
    count = secs * tiles
    me = lax.axis_index("sec") * tiles + lax.axis_index("tile")
    right, left = lax.rem(me + 1, count), lax.rem(me + count - 1, count)

    def place(device):
        return (device // tiles, lax.rem(device, tiles))

    width = atm_ref.shape[1]
    ocean_count = cols_hbm.shape[1]
    bands, columns_n = temp_ref.shape
    across = columns_n // LANES
    sides = (right, left)
    there = (me < count - 1, me > 0)
    slabs = list(windows) + [last]

    def own_copy(j):
        return pltpu.make_async_copy(
            atm_ref.at[pl.ds(STARTS[j], CHUNKS[j])],
            slabs[j].at[:, pl.ds(width, width)],
            own_sem.at[j],
        )

    def weight_copy(p):
        part = ocean_count // WEIGHT_PARTS
        return pltpu.make_async_copy(
            blocks_ref.at[pl.ds(p * part, part)],
            weights.at[pl.ds(p * part, part)],
            weight_sem.at[p],
        )

    def bulk_copy(j, side):
        return pltpu.make_async_remote_copy(
            src_ref=atm_ref.at[pl.ds(STARTS[j], CHUNKS[j])],
            dst_ref=slabs[j].at[:, pl.ds(2 * width * side, width)],
            send_sem=bulk_send.at[side, j],
            recv_sem=bulk_recv.at[side, j],
            device_id=place(sides[side]),
            device_id_type=MESH,
        )

    def edge_copy(step, side):
        source, target = ((edge_out, edge_in), (edge2_out, edge2_in))[step]
        return pltpu.make_async_remote_copy(
            src_ref=source.at[side],
            dst_ref=target.at[side],
            send_sem=edge_send.at[step, side],
            recv_sem=edge_recv.at[step, side],
            device_id=place(sides[1 - side]),
            device_id_type=MESH,
        )

    odd = lax.rem(me, 2) == 1
    def held(device):
        tile = lax.rem(device, tiles)
        return ((lax.rem(tile, 4) == 0) & (tile > 0)) | ((lax.rem(tile, 4) == 3) & (tile < tiles - 1))

    waits = held(me)
    partner = me + 1 - 2 * lax.rem(me, 2)
    outward = (there[0] & odd, there[1] & ~odd)
    inward = (there[0] & ~odd, there[1] & odd)

    def send_off(j):
        for side in range(2):
            pl.when(outward[side])(bulk_copy(j, side).start)

    def send(j, late=True):
        if late:
            send_off(j)
        for side in range(2):
            pl.when(inward[side])(bulk_copy(j, side).start)

    barrier = pltpu.get_barrier_semaphore()
    for side in range(2):

        @pl.when(there[side])
        def _():
            pl.semaphore_signal(barrier, inc=1, device_id=place(sides[side]), device_id_type=MESH)

    smalls = [
        pltpu.make_async_copy(source, target, small_sem.at[i])
        for i, (source, target) in enumerate(
            ((temp_hbm, temp_ref), (sea_hbm, sea_ref), (cols_hbm, named_ref), (flux_hbm, flux_ref))
        )
    ]
    for copy in smalls:
        copy.start()
    pl.semaphore_wait(barrier, jnp.where((me == 0) | (me == count - 1), 1, 2))
    send(0)
    for j in range(len(CHUNKS)):
        own_copy(j).start()
    for copy in smalls:
        copy.wait()
    land = sea_ref[...].astype(jnp.float32)
    edge_out[0, 0:1, :] = temp_ref[0:1, :]
    edge_out[0, 1:2, :] = land[0:1, :]
    edge_out[1, 0:1, :] = temp_ref[bands - 1 : bands, :]
    edge_out[1, 1:2, :] = land[bands - 1 : bands, :]
    for side in range(2):
        pl.when(there[1 - side])(edge_copy(0, side).start)
    for j in range(1, HALF):
        send(j)
    for p in range(WEIGHT_PARTS):
        weight_copy(p).start()
    for j in range(HALF, len(CHUNKS)):
        send(j, late=False)
    pl.when(~waits)(lambda: send_off(HALF))
    temp[...] = jnp.zeros_like(temp)
    sea[...] = jnp.zeros_like(sea)
    temp[1 : 1 + bands, :] = temp_ref[...]
    sea[1 : 1 + bands, :] = land
    fill_coef(coef, flux_ref)
    for total in (forcing0, forcing1, air0, air1):
        total[...] = jnp.zeros_like(total)

    base = (me - 1) * (width // LANES)

    def locate(t, carry):
        for k in range(cols_ref.shape[0]):
            cols_ref[k, t] = jnp.clip(named_ref[k, t] - base, 0, 3 * (width // LANES) - 1)
        return carry

    lax.fori_loop(0, ocean_count, locate, 0, unroll=4)

    def first_sweep():
        for side in range(2):
            pl.when(there[side])(edge_copy(0, side).wait_recv)
        temp[0:1, :] = jnp.where(there[1], edge_in[1, 0:1, :], 0.0)
        temp[1 + bands : 2 + bands, :] = jnp.where(there[0], edge_in[0, 0:1, :], 0.0)
        sea[0:1, :] = jnp.where(there[1], edge_in[1, 1:2, :], 0.0)
        sea[1 + bands : 2 + bands, :] = jnp.where(there[0], edge_in[0, 1:2, :], 0.0)
        land = sea[...]
        masks[0] = pltpu.roll(land, 7, 0)
        masks[1] = pltpu.roll(land, 1, 0)
        masks[2] = pltpu.roll(land, columns_n - 1, 1)
        masks[3] = pltpu.roll(land, 1, 1)
        new = sweep(temp[...], sea[...], masks, forcing0[...], air0[...])
        edge2_out[0] = new[1:2, :]
        edge2_out[1] = new[bands : 1 + bands, :]
        for side in range(2):
            pl.when(there[1 - side])(edge_copy(1, side).start)
        temp[...] = new

    for p in range(WEIGHT_PARTS):
        weight_copy(p).wait()
    for j in range(EARLY):
        own_copy(j).wait()
        for side in range(2):
            pl.when(there[1 - side])(bulk_copy(j, side).wait_recv)
        if j == HALF - 1:

            @pl.when(held(partner))
            def _():
                pl.semaphore_signal(turn_sem, inc=1, device_id=place(partner), device_id_type=MESH)

        def store(t, value):
            ocean[STARTS[j] : STARTS[j] + CHUNKS[j], pl.ds(pl.multiple_of(t * LANES, LANES), LANES)] = value

        early = STARTS[j] < 2 * fields_n
        remap_rows(
            CHUNKS[j], STARTS[j] % fields_n, across, bands, cols_ref, slabs[j], weights, coef,
            store, forcing0 if early else forcing1, air0 if early else air1,
        )
        if STARTS[j] + CHUNKS[j] == 2 * fields_n:
            first_sweep()

            @pl.when(waits)
            def _():
                pl.semaphore_wait(turn_sem, 1)
                send_off(HALF)

            for later in range(HALF + 1, len(CHUNKS)):
                send_off(later)

    for side in range(2):
        pl.when(there[side])(edge_copy(1, side).wait_recv)
    temp[0:1, :] = jnp.where(there[1], edge2_in[1], 0.0)
    temp[1 + bands : 2 + bands, :] = jnp.where(there[0], edge2_in[0], 0.0)
    for step in range(2):
        for side in range(2):
            pl.when(there[1 - side])(edge_copy(step, side).wait_send)
    own_copy(EARLY).wait()
    for j in range(len(CHUNKS)):
        for side in range(2):
            pl.when(there[side])(bulk_copy(j, side).wait_send)
    for side in range(2):
        pl.when(there[1 - side])(bulk_copy(EARLY, side).wait_recv)


def finish_kernel(
    fields_n, cols_ref, weights, ocean, last, temp, sea, masks, forcing_in, air, coef,
    out_ref, final_ref,
    forcing, late, final, sems,
):
    bands, columns_n = final.shape
    across = columns_n // LANES
    early = pltpu.make_async_copy(ocean, out_ref.at[pl.ds(0, STARTS[EARLY])], sems.at[0])
    early.start()
    forcing[...] = forcing_in[...]

    def store(t, value):
        late[:, pl.ds(pl.multiple_of(t * LANES, LANES), LANES)] = value

    remap_rows(
        CHUNKS[EARLY], STARTS[EARLY] % fields_n, across, bands, cols_ref, last, weights, coef,
        store, forcing, None,
    )
    rest = pltpu.make_async_copy(late, out_ref.at[pl.ds(STARTS[EARLY], CHUNKS[EARLY])], sems.at[1])
    rest.start()
    final[...] = sweep(temp[...], sea[...], masks, forcing[...], air[...])[1 : 1 + bands, :]
    done = pltpu.make_async_copy(final, final_ref, sems.at[2])
    done.start()
    early.wait()
    rest.wait()
    done.wait()


def solution(mesh):
    secs, tiles = mesh.shape["sec"], mesh.shape["tile"]

    def body(atm_fields, remap_blocks, block_cols, flux_coef, ocean_temp, sea_mask):
        rows_n, width = atm_fields.shape
        ocean_count, slots = block_cols.shape
        bands, columns_n = ocean_temp.shape
        fields_n = flux_coef.shape[0]
        chunks = len(CHUNKS)
        blocks = remap_blocks.reshape(ocean_count, slots * LANES, LANES)
        vmem = pl.BlockSpec(memory_space=pltpu.VMEM)
        smem = pl.BlockSpec(memory_space=pltpu.SMEM)
        hbm = pl.BlockSpec(memory_space=pltpu.HBM)
        grid_state = (8, columns_n)
        inputs = [
            pltpu.with_memory_space_constraint(x, pltpu.HBM)
            for x in (block_cols.T, flux_coef, atm_fields, blocks, ocean_temp, sea_mask)
        ]
        state = pl.pallas_call(
            functools.partial(exchange_kernel, secs, tiles, fields_n),
            out_shape=(
                pltpu.VMEM(blocks.shape, jnp.bfloat16),
                pltpu.VMEM((STARTS[EARLY], ocean_count * LANES), jnp.bfloat16),
                pltpu.VMEM((CHUNKS[EARLY], 3 * width), jnp.bfloat16),
                pltpu.VMEM(grid_state, jnp.float32),
                pltpu.VMEM(grid_state, jnp.float32),
                pltpu.VMEM((4,) + grid_state, jnp.float32),
                pltpu.VMEM(grid_state, jnp.float32),
                pltpu.VMEM(grid_state, jnp.float32),
                pltpu.VMEM((fields_n, LANES), jnp.float32),
                pltpu.SMEM((slots, ocean_count), jnp.int32),
            ),
            in_specs=[hbm] * 6,
            out_specs=[vmem] * 9 + [smem],
            scratch_shapes=[
                pltpu.SMEM((slots, ocean_count), jnp.int32),
                pltpu.SMEM((fields_n,), jnp.float32),
                pltpu.VMEM((bands, columns_n), jnp.float32),
                pltpu.VMEM((bands, columns_n), jnp.int32),
                [pltpu.VMEM((r, 3 * width), jnp.bfloat16) for r in CHUNKS[:EARLY]],
                pltpu.VMEM(grid_state, jnp.float32),
                pltpu.VMEM(grid_state, jnp.float32),
                pltpu.VMEM((2, 2, columns_n), jnp.float32),
                pltpu.VMEM((2, 2, columns_n), jnp.float32),
                pltpu.VMEM((2, 1, columns_n), jnp.float32),
                pltpu.VMEM((2, 1, columns_n), jnp.float32),
                pltpu.SemaphoreType.DMA((4,)),
                pltpu.SemaphoreType.DMA((chunks,)),
                pltpu.SemaphoreType.DMA((WEIGHT_PARTS,)),
                pltpu.SemaphoreType.DMA((2, chunks)),
                pltpu.SemaphoreType.DMA((2, chunks)),
                pltpu.SemaphoreType.DMA((2, 2)),
                pltpu.SemaphoreType.DMA((2, 2)),
                pltpu.SemaphoreType.REGULAR,
            ],
            compiler_params=pltpu.CompilerParams(
                collective_id=0, has_side_effects=True, vmem_limit_bytes=16 << 20
            ),
            name="exchange",
        )(*inputs)
        weights, ocean, last, temp, sea, masks, forcing, air, coef, cols = state
        kept = [
            pltpu.with_memory_space_constraint(x, pltpu.VMEM)
            for x in (weights, ocean, last, temp, sea, masks, forcing, air, coef)
        ]
        return pl.pallas_call(
            functools.partial(finish_kernel, fields_n),
            out_shape=(
                pltpu.HBM((rows_n, ocean_count * LANES), jnp.bfloat16),
                pltpu.HBM((bands, columns_n), jnp.float32),
            ),
            in_specs=[smem] + [vmem] * 9,
            out_specs=(hbm, hbm),
            scratch_shapes=[
                pltpu.VMEM(grid_state, jnp.float32),
                pltpu.VMEM((CHUNKS[EARLY], ocean_count * LANES), jnp.bfloat16),
                pltpu.VMEM((bands, columns_n), jnp.float32),
                pltpu.SemaphoreType.DMA((3,)),
            ],
            compiler_params=pltpu.CompilerParams(vmem_limit_bytes=8 << 20),
            name="finish",
        )(pltpu.with_memory_space_constraint(cols, pltpu.SMEM), *kept)

    band = P(("sec", "tile"), None)
    return jax.shard_map(
        body,
        mesh=mesh,
        in_specs=(P(None, ("sec", "tile")), P(("sec", "tile"), None, None, None), band, P(), band, band),
        out_specs=(P(None, ("sec", "tile")), band),
        check_vma=False,
    )
```

time: 101 us -> 32.2 us (0.32)
  the two profiles are of different devices: /device:TPU:16 before, /device:TPU:193 now
where the time goes in v1:
time: 32.2 us; the launch traced here: 32 us
  Pallas kernels  31.4 us (98%)
  between operations  0.64 us (2%)
    pallas_call x1, Pallas kernels, body(): pl.pallas_call(functools.partial(exchange_kernel, secs, tiles, fields_n),...  28.8 us
    pallas_call x1, Pallas kernels, body(): pl.pallas_call(functools.partial(finish_kernel, fields_n), out_shape=(plt...  2.53 us

profile of v1, /device:TPU:193, one launch (start us, length us, event | category | flops | bytes accessed | tf_op | source)
XLA Modules:
  0.0 32.0 jit_solution(12469020962434037666)
XLA Ops:
  0.6 28.8 %exchange.1 = (bf16[64,512,128]{2,1,0:T(8,128)(2,1)S(1)}, bf16[112,8192]{1,0:T(8,128)(2,1)S(1)}, bf16[16,12288]{1,0:T(8,128)(2,1)S(1)}, f32[8,2048]{1,0:T(8,128)...) custom-call(s32[4,64]{1,0:T(4,128)} %bitcast.3, ...), custom_call_target="tpu_custom_call" | custom-call | tf_op jit(solution)/shard_map/exchange/pallas_call | solution.py:311
  29.5 2.5 %finish.1 = (bf16[128,8192]{1,0:T(8,128)(2,1)}, f32[4,2048]{1,0:T(4,128)}) custom-call(s32[4,64]{1,0:T(4,128)S(4)} %get-tuple-element.12.cols_ref, bf16[64,512,128]{2,1,0:T(8,128)(2,1)S(1)} %get-tuple-element.13.weights, bf16[112,8192]{1,0:T(8,128)(2,1)S(1)} %get-tuple-element.14.ocean, bf16[16,12288]{1,0:T(8,128)(2,1)S(1)} %get-tuple-element.15.last, ...), custom_call_target="tpu_custom_call" | custom-call | tf_op jit(solution)/shard_map/finish/pallas_call | solution.py:358

commit v2 on v1

--- a/solution.py
+++ b/solution.py
@@ -24,31 +24,27 @@
         coef[f : f + 1, :] = jnp.full((1, LANES), 0.5 * flux_ref[f], jnp.float32)
 
 
-def remap_rows(rows, first, across, bands, cols_ref, window, weights, coef, store, forcing, air):
+def remap_rows(rows, first, band, cols_ref, window, weights, coef, store, add):
     slots = cols_ref.shape[0]
+    bands, columns_n = band
+    across = columns_n // LANES
 
     def column(xt, carry):
         heat, warm = [], []
         for y in range(bands):
             t = y * across + xt
             picked = jnp.concatenate(
-                [
-                    window[:, pl.ds(cols_ref[k, t] * LANES, LANES)]
-                    for k in range(slots)
-                ],
-                axis=1,
+                [window[:, pl.ds(cols_ref[k, t] * LANES, LANES)] for k in range(slots)], axis=1
             )
             total = jnp.dot(picked, weights[t], preferred_element_type=jnp.float32)
             store(t, total.astype(jnp.bfloat16))
             heat.append(jnp.sum(total * coef[first : first + rows, :], axis=0, keepdims=True))
-            if first == 0:
-                warm.append(0.5 * total[0:1, :])
-        lanes = pl.ds(pl.multiple_of(xt * LANES, LANES), LANES)
-        top = jnp.zeros((1, LANES), jnp.float32)
-        low = jnp.zeros((8 - 1 - bands, LANES), jnp.float32)
-        forcing[:, lanes] += jnp.concatenate([top] + heat + [low], axis=0)
-        if first == 0:
-            air[:, lanes] += jnp.concatenate([top] + warm + [low], axis=0)
+            warm.append(0.5 * total[0:1, :])
+        add(
+            pl.ds(pl.multiple_of(xt * LANES, LANES), LANES),
+            jnp.concatenate(heat, axis=0),
+            jnp.concatenate(warm, axis=0) if first == 0 else None,
+        )
         return carry
 
     lax.fori_loop(0, across, column, 0, unroll=across)
@@ -69,8 +65,8 @@
 
 def exchange_kernel(
     secs, tiles, fields_n, cols_hbm, flux_hbm, atm_ref, blocks_ref, temp_hbm, sea_hbm,
-    weights, ocean, last, temp, sea, masks, forcing1, air1, coef, cols_ref,
-    named_ref, flux_ref, temp_ref, sea_ref, windows, forcing0, air0,
+    weights, ocean, last, base, sea_out, coef, cols_ref,
+    named_ref, flux_ref, temp_ref, sea_ref, windows, temp, sea, masks, forcing0, air0, forcing1, air1,
     edge_out, edge_in, edge2_out, edge2_in,
     small_sem, own_sem, weight_sem, bulk_send, bulk_recv, edge_send, edge_recv, turn_sem,
 ):
@@ -180,6 +176,7 @@
     for j in range(HALF, len(CHUNKS)):
         send(j, late=False)
     pl.when(~waits)(lambda: send_off(HALF))
+    pl.when(~waits)(lambda: send_off(HALF + 1))
     temp[...] = jnp.zeros_like(temp)
     sea[...] = jnp.zeros_like(sea)
     temp[1 : 1 + bands, :] = temp_ref[...]
@@ -188,11 +185,11 @@
     for total in (forcing0, forcing1, air0, air1):
         total[...] = jnp.zeros_like(total)
 
-    base = (me - 1) * (width // LANES)
+    lowest = (me - 1) * (width // LANES)
 
     def locate(t, carry):
         for k in range(cols_ref.shape[0]):
-            cols_ref[k, t] = jnp.clip(named_ref[k, t] - base, 0, 3 * (width // LANES) - 1)
+            cols_ref[k, t] = jnp.clip(named_ref[k, t] - lowest, 0, 3 * (width // LANES) - 1)
         return carry
 
     lax.fori_loop(0, ocean_count, locate, 0, unroll=4)
@@ -232,9 +229,15 @@
             ocean[STARTS[j] : STARTS[j] + CHUNKS[j], pl.ds(pl.multiple_of(t * LANES, LANES), LANES)] = value
 
         early = STARTS[j] < 2 * fields_n
+        forcing, air = (forcing0, air0) if early else (forcing1, air1)
+
+        def add(lanes, heat, warm):
+            forcing[1 : 1 + bands, lanes] += heat
+            if warm is not None:
+                air[1 : 1 + bands, lanes] += warm
+
         remap_rows(
-            CHUNKS[j], STARTS[j] % fields_n, across, bands, cols_ref, slabs[j], weights, coef,
-            store, forcing0 if early else forcing1, air0 if early else air1,
+            CHUNKS[j], STARTS[j] % fields_n, (bands, columns_n), cols_ref, slabs[j], weights, coef, store, add
         )
         if STARTS[j] + CHUNKS[j] == 2 * fields_n:
             first_sweep()
@@ -243,14 +246,17 @@
             def _():
                 pl.semaphore_wait(turn_sem, 1)
                 send_off(HALF)
-
-            for later in range(HALF + 1, len(CHUNKS)):
+                send_off(HALF + 1)
+
+            for later in range(HALF + 2, len(CHUNKS)):
                 send_off(later)
 
     for side in range(2):
         pl.when(there[side])(edge_copy(1, side).wait_recv)
     temp[0:1, :] = jnp.where(there[1], edge2_in[1], 0.0)
     temp[1 + bands : 2 + bands, :] = jnp.where(there[0], edge2_in[0], 0.0)
+    base[...] = sweep(temp[...], sea[...], masks, forcing1[...], air1[...])[1 : 1 + bands, :]
+    sea_out[...] = sea_ref[...].astype(jnp.float32)
     for step in range(2):
         for side in range(2):
             pl.when(there[1 - side])(edge_copy(step, side).wait_send)
@@ -263,29 +269,30 @@
 
 
 def finish_kernel(
-    fields_n, cols_ref, weights, ocean, last, temp, sea, masks, forcing_in, air, coef,
-    out_ref, final_ref,
-    forcing, late, final, sems,
+    fields_n, cols_ref, weights, ocean, last, base, sea, coef, out_ref, final_ref, late, final, sems
 ):
-    bands, columns_n = final.shape
-    across = columns_n // LANES
-    early = pltpu.make_async_copy(ocean, out_ref.at[pl.ds(0, STARTS[EARLY])], sems.at[0])
-    early.start()
-    forcing[...] = forcing_in[...]
+    step = CHUNKS[EARLY]
+
+    def early(i):
+        rows = pl.ds(pl.multiple_of(i * step, step), step)
+        return pltpu.make_async_copy(ocean.at[rows], out_ref.at[rows], sems.at[2 + i])
+
+    lax.fori_loop(0, STARTS[EARLY] // step, lambda i, carry: (early(i).start(), carry)[1], 0)
 
     def store(t, value):
         late[:, pl.ds(pl.multiple_of(t * LANES, LANES), LANES)] = value
 
+    def add(lanes, heat, warm):
+        final[:, lanes] = base[:, lanes] + sea[:, lanes] * (TIMESTEP * heat)
+
     remap_rows(
-        CHUNKS[EARLY], STARTS[EARLY] % fields_n, across, bands, cols_ref, last, weights, coef,
-        store, forcing, None,
+        CHUNKS[EARLY], STARTS[EARLY] % fields_n, final.shape, cols_ref, last, weights, coef, store, add
     )
-    rest = pltpu.make_async_copy(late, out_ref.at[pl.ds(STARTS[EARLY], CHUNKS[EARLY])], sems.at[1])
+    rest = pltpu.make_async_copy(late, out_ref.at[pl.ds(STARTS[EARLY], step)], sems.at[0])
     rest.start()
-    final[...] = sweep(temp[...], sea[...], masks, forcing[...], air[...])[1 : 1 + bands, :]
-    done = pltpu.make_async_copy(final, final_ref, sems.at[2])
+    done = pltpu.make_async_copy(final, final_ref, sems.at[1])
     done.start()
-    early.wait()
+    lax.fori_loop(0, STARTS[EARLY] // step, lambda i, carry: (early(i).wait(), carry)[1], 0)
     rest.wait()
     done.wait()
 
@@ -314,22 +321,24 @@
                 pltpu.VMEM(blocks.shape, jnp.bfloat16),
                 pltpu.VMEM((STARTS[EARLY], ocean_count * LANES), jnp.bfloat16),
                 pltpu.VMEM((CHUNKS[EARLY], 3 * width), jnp.bfloat16),
-                pltpu.VMEM(grid_state, jnp.float32),
-                pltpu.VMEM(grid_state, jnp.float32),
-                pltpu.VMEM((4,) + grid_state, jnp.float32),
-                pltpu.VMEM(grid_state, jnp.float32),
-                pltpu.VMEM(grid_state, jnp.float32),
+                pltpu.VMEM((bands, columns_n), jnp.float32),
+                pltpu.VMEM((bands, columns_n), jnp.float32),
                 pltpu.VMEM((fields_n, LANES), jnp.float32),
                 pltpu.SMEM((slots, ocean_count), jnp.int32),
             ),
             in_specs=[hbm] * 6,
-            out_specs=[vmem] * 9 + [smem],
+            out_specs=[vmem] * 6 + [smem],
             scratch_shapes=[
                 pltpu.SMEM((slots, ocean_count), jnp.int32),
                 pltpu.SMEM((fields_n,), jnp.float32),
                 pltpu.VMEM((bands, columns_n), jnp.float32),
                 pltpu.VMEM((bands, columns_n), jnp.int32),
                 [pltpu.VMEM((r, 3 * width), jnp.bfloat16) for r in CHUNKS[:EARLY]],
+                pltpu.VMEM(grid_state, jnp.float32),
+                pltpu.VMEM(grid_state, jnp.float32),
+                pltpu.VMEM((4,) + grid_state, jnp.float32),
+                pltpu.VMEM(grid_state, jnp.float32),
+                pltpu.VMEM(grid_state, jnp.float32),
                 pltpu.VMEM(grid_state, jnp.float32),
                 pltpu.VMEM(grid_state, jnp.float32),
                 pltpu.VMEM((2, 2, columns_n), jnp.float32),
@@ -350,28 +359,23 @@
             ),
             name="exchange",
         )(*inputs)
-        weights, ocean, last, temp, sea, masks, forcing, air, coef, cols = state
-        kept = [
-            pltpu.with_memory_space_constraint(x, pltpu.VMEM)
-            for x in (weights, ocean, last, temp, sea, masks, forcing, air, coef)
-        ]
+        kept = [pltpu.with_memory_space_constraint(x, pltpu.VMEM) for x in state[:-1]]
         return pl.pallas_call(
             functools.partial(finish_kernel, fields_n),
             out_shape=(
                 pltpu.HBM((rows_n, ocean_count * LANES), jnp.bfloat16),
                 pltpu.HBM((bands, columns_n), jnp.float32),
             ),
-            in_specs=[smem] + [vmem] * 9,
+            in_specs=[smem] + [vmem] * 6,
             out_specs=(hbm, hbm),
             scratch_shapes=[
-                pltpu.VMEM(grid_state, jnp.float32),
                 pltpu.VMEM((CHUNKS[EARLY], ocean_count * LANES), jnp.bfloat16),
                 pltpu.VMEM((bands, columns_n), jnp.float32),
-                pltpu.SemaphoreType.DMA((3,)),
+                pltpu.SemaphoreType.DMA((2 + STARTS[EARLY] // CHUNKS[EARLY],)),
             ],
             compiler_params=pltpu.CompilerParams(vmem_limit_bytes=8 << 20),
             name="finish",
-        )(pltpu.with_memory_space_constraint(cols, pltpu.SMEM), *kept)
+        )(pltpu.with_memory_space_constraint(state[-1], pltpu.SMEM), *kept)
 
     band = P(("sec", "tile"), None)
     return jax.shard_map(

time: 32.2 us -> 30.5 us (0.947)
  the two profiles are of different devices: /device:TPU:193 before, /device:TPU:1 now
where the time goes in v2:
time: 30.5 us; the launch traced here: 30.4 us
  Pallas kernels  29.7 us (97%)
  between operations  0.64 us (2%)
    pallas_call x1, Pallas kernels, body(): pl.pallas_call(functools.partial(exchange_kernel, secs, tiles, fields_n),...  27.6 us
    pallas_call x1, Pallas kernels, body(): pl.pallas_call(functools.partial(finish_kernel, fields_n), out_shape=(plt...  2.13 us

profile of v2, /device:TPU:1, one launch (start us, length us, event | category | flops | bytes accessed | tf_op | source)
XLA Modules:
  0.0 30.4 jit_solution(3813180533057844927)
XLA Ops:
  0.6 27.6 %exchange.1 = (bf16[64,512,128]{2,1,0:T(8,128)(2,1)S(1)}, bf16[112,8192]{1,0:T(8,128)(2,1)S(1)}, bf16[16,12288]{1,0:T(8,128)(2,1)S(1)}, f32[4,2048]{1,0:T(4,128)...) custom-call(s32[4,64]{1,0:T(4,128)} %bitcast.3, f32[32]{0:T(128)} %flux_hbm.1, ...), custom_call_target="tpu_custom_call" | custom-call | tf_op jit(solution)/shard_map/exchange/pallas_call | solution.py:318
  28.3 2.1 %finish.1 = (bf16[128,8192]{1,0:T(8,128)(2,1)}, f32[4,2048]{1,0:T(4,128)}) custom-call(s32[4,64]{1,0:T(4,128)S(4)} %get-tuple-element.9.cols_ref, bf16[64,512,128]{2,1,0:T(8,128)(2,1)S(1)} %get-tuple-element.10.weights, bf16[112,8192]{1,0:T(8,128)(2,1)S(1)} %get-tuple-element.11.ocean, bf16[16,12288]{1,0:T(8,128)(2,1)S(1)} %get-tuple-element.12.last, ...), custom_call_target="tpu_custom_call" | custom-call | tf_op jit(solution)/shard_map/finish/pallas_call | solution.py:363

commit v3 on v2

--- a/solution.py
+++ b/solution.py
@@ -124,10 +124,11 @@
     odd = lax.rem(me, 2) == 1
     def held(device):
         tile = lax.rem(device, tiles)
-        return ((lax.rem(tile, 4) == 0) & (tile > 0)) | ((lax.rem(tile, 4) == 3) & (tile < tiles - 1))
+        return ((lax.rem(tile, 4) == 0) & (lax.rem(tile, 16) > 0)) | ((lax.rem(tile, 4) == 3) & (lax.rem(tile, 16) < 15))
 
     waits = held(me)
     partner = me + 1 - 2 * lax.rem(me, 2)
+    eager = ~waits & ~held(partner)
     outward = (there[0] & odd, there[1] & ~odd)
     inward = (there[0] & ~odd, there[1] & odd)
 
@@ -177,6 +178,7 @@
         send(j, late=False)
     pl.when(~waits)(lambda: send_off(HALF))
     pl.when(~waits)(lambda: send_off(HALF + 1))
+    pl.when(eager)(lambda: send_off(EARLY))
     temp[...] = jnp.zeros_like(temp)
     sea[...] = jnp.zeros_like(sea)
     temp[1 : 1 + bands, :] = temp_ref[...]
@@ -248,8 +250,7 @@
                 send_off(HALF)
                 send_off(HALF + 1)
 
-            for later in range(HALF + 2, len(CHUNKS)):
-                send_off(later)
+            pl.when(~eager)(lambda: send_off(EARLY))
 
     for side in range(2):
         pl.when(there[side])(edge_copy(1, side).wait_recv)

time: 30.5 us -> 30.5 us (level)
  no operation moved by 1% of the time
where the time goes in v3:
time: 30.5 us; the launch traced here: 30.3 us
  Pallas kernels  29.7 us (97%)
  between operations  0.64 us (2%)
    pallas_call x1, Pallas kernels, body(): pl.pallas_call(functools.partial(exchange_kernel, secs, tiles, fields_n),...  27.6 us
    pallas_call x1, Pallas kernels, body(): pl.pallas_call(functools.partial(finish_kernel, fields_n), out_shape=(plt...  2.14 us

profile of v3, /device:TPU:1, one launch (start us, length us, event | category | flops | bytes accessed | tf_op | source)
XLA Modules:
  0.0 30.3 jit_solution(3389348984618000121)
XLA Ops:
  0.6 27.6 %exchange.1 = (bf16[64,512,128]{2,1,0:T(8,128)(2,1)S(1)}, bf16[112,8192]{1,0:T(8,128)(2,1)S(1)}, bf16[16,12288]{1,0:T(8,128)(2,1)S(1)}, f32[4,2048]{1,0:T(4,128)...) custom-call(s32[4,64]{1,0:T(4,128)} %bitcast.3, f32[32]{0:T(128)} %flux_hbm.1, ...), custom_call_target="tpu_custom_call" | custom-call | tf_op jit(solution)/shard_map/exchange/pallas_call | solution.py:319
  28.2 2.1 %finish.1 = (bf16[128,8192]{1,0:T(8,128)(2,1)}, f32[4,2048]{1,0:T(4,128)}) custom-call(s32[4,64]{1,0:T(4,128)S(4)} %get-tuple-element.9.cols_ref, bf16[64,512,128]{2,1,0:T(8,128)(2,1)S(1)} %get-tuple-element.10.weights, bf16[112,8192]{1,0:T(8,128)(2,1)S(1)} %get-tuple-element.11.ocean, bf16[16,12288]{1,0:T(8,128)(2,1)S(1)} %get-tuple-element.12.last, ...), custom_call_target="tpu_custom_call" | custom-call | tf_op jit(solution)/shard_map/finish/pallas_call | solution.py:364
